TPU v7x, 512 devices: a whole 4x8x8 slice. The times are simulated.
512 devices in a mesh: row: 8 (over z), col: 16 (over y, core), depth: 4 (over x).
Axes of the slice: x: 4, y: 8, z: 8, core: 2. Of those that a mesh axis runs over, the one named last changes fastest.
Arguments:
- tokens: bfloat16 [4096, 8192], P(('row', 'col'), 'depth'), may hold values from -6 to 6
- gate_weight: bfloat16 [8192, 14336], P(('depth', 'row'), 'col'), may hold values from -0.0625 to 0.0625
- up_weight: bfloat16 [8192, 14336], P(('depth', 'row'), 'col'), may hold values from -0.0625 to 0.0625
- down_weight: bfloat16 [14336, 8192], P(('col', 'row'), 'depth'), may hold values from -0.125 to 0.125
- gate_keep: int32 [64, 112], replicated, may hold values from 0 to 1, as said below
- up_keep: int32 [64, 112], replicated, may hold values from 0 to 1, as said below
- down_keep: int32 [112, 64], replicated, may hold values from 0 to 1, as said below
Outputs:
- mixed: bfloat16 [4096, 8192], P(('row', 'col'), 'depth')
Inputs may be any that keep to these rules, and one draw needn't show every extreme that they name: `gate_keep`: 1 marks a kept block of the gate projection, 0 a dropped one. `up_keep`: 1 marks a kept block of the up projection, 0 a dropped one. `down_keep`: 1 marks a kept block of the down projection, 0 a dropped one.
All inputs are finite; a program needn't handle non-finite values.
Results may differ from a plain program's by a relative error of at most 0.005.
Values may be sent and summed in bfloat16 or wider, within the bound.
No kernel may reach another device: no remote copies, remote signals or barrier semaphores. Data moves between devices by JAX's collectives and lax.ppermute only.
A program may use at most 64 MiB of HBM per device.

v0:
```python
import jax
import jax.numpy as jnp
from jax import lax
from jax.sharding import PartitionSpec as P

BLOCK = 128


def keep_table(keep, row_start, col_start, row_count, col_count):
    keep_bits = keep.astype(jnp.bfloat16)
    row_ids = (row_start + jnp.arange(row_count, dtype=jnp.int32)) // BLOCK
    col_ids = (col_start + jnp.arange(col_count, dtype=jnp.int32)) // BLOCK
    pick_rows = (row_ids[:, None] == jnp.arange(keep.shape[0], dtype=jnp.int32)[None, :]).astype(
        jnp.bfloat16
    )
    pick_cols = (jnp.arange(keep.shape[1], dtype=jnp.int32)[:, None] == col_ids[None, :]).astype(
        jnp.bfloat16
    )
    inner = jnp.dot(keep_bits, pick_cols, preferred_element_type=jnp.float32).astype(jnp.bfloat16)
    return jnp.dot(pick_rows, inner, preferred_element_type=jnp.float32).astype(jnp.bfloat16)


def add_panel(token_block, piece):
    return jnp.dot(token_block, piece, preferred_element_type=jnp.float32)


def on_device(tokens, gate_weight, up_weight, down_weight, gate_keep, up_keep, down_keep):
    depth_pos = lax.axis_index("depth")
    row_pos = lax.axis_index("row")
    column_pos = lax.axis_index("col")
    row_total = lax.axis_size("row")
    feature_rows = gate_weight.shape[0]
    hidden_cols = gate_weight.shape[1]
    feature_start = (depth_pos * row_total + row_pos) * feature_rows
    hidden_start = column_pos * hidden_cols
    gate_masked = gate_weight * keep_table(
        gate_keep, feature_start, hidden_start, feature_rows, hidden_cols
    )
    up_masked = up_weight * keep_table(
        up_keep, feature_start, hidden_start, feature_rows, hidden_cols
    )
    down_rows_count = down_weight.shape[0]
    down_features = down_weight.shape[1]
    down_start = (column_pos * row_total + row_pos) * down_rows_count
    down_masked = down_weight * keep_table(
        down_keep, down_start, depth_pos * down_features, down_rows_count, down_features
    )
    token_block = lax.all_gather(tokens, "col", axis=0, tiled=True)

    def add_one(piece):
        return add_panel(token_block, piece)

    gate = add_one(lax.all_gather(gate_masked, "row", axis=0, tiled=True))
    up = add_one(lax.all_gather(up_masked, "row", axis=0, tiled=True))
    both = jnp.stack((gate, up), 0)
    total = lax.psum(both, "depth")
    hidden = (jax.nn.silu(total[0]) * total[1]).astype(jnp.bfloat16)
    down_block = lax.all_gather(down_masked, "row", axis=0, tiled=True)
    mixed = lax.psum_scatter(
        jnp.dot(hidden, down_block, preferred_element_type=jnp.float32),
        "col",
        scatter_dimension=0,
        tiled=True,
    )
    return mixed.astype(jnp.bfloat16)


def solution(mesh):
    placed = (
        P(("row", "col"), "depth"),
        P(("depth", "row"), "col"),
        P(("depth", "row"), "col"),
        P(("col", "row"), "depth"),
        P(),
        P(),
        P(),
    )
    return jax.shard_map(
        on_device, mesh=mesh, in_specs=placed, out_specs=P(("row", "col"), "depth"), check_vma=False
    )
```

profile of v0, /device:TPU:25, one launch (start us, length us, event | category | flops | bytes accessed | tf_op | source)
XLA Modules:
  0.0 393.9 jit_solution(8674119538249657588)
XLA Ops:
  6.5 0.0 copy-start
  6.5 0.0 copy-start.1
  6.5 0.0 all-gather.7.cloned.1.call-start
  6.5 0.7 all-gather.7.cloned.1.call-update
  7.3 0.0 all-gather.9.cloned.1.call-start
  7.4 2.3 fusion.4
  9.7 0.0 all-gather.9.cloned.1.call-update
  9.7 0.0 all-gather.5.cloned.1.call-start
  9.8 2.3 fusion.3
  12.1 0.0 all-gather.5.cloned.1.call-update
  12.1 0.0 all-gather.11.cloned.1.call-start
  12.2 0.0 copy-done
  12.2 0.0 copy-done.1
  12.2 1.4 fusion
  13.7 0.0 all-gather.11.cloned.1.call-update
  13.7 0.0 all-reduce.2.cloned.1.call-start
  13.7 42.2 %all-gather.7.cloned.1.call-done = bf16[512,2048]{1,0:T(8,128)(2,1)} async-done(((bf16[32,2048]{1,0:T(8,128)(2,1)}), bf16[512,2048]{1,0:T(8,128)(2,1)}) %all-gather.7.cloned.1.call-update) | async-done | bytes 2097168 | tf_op jit(solution)/shard_map/all_gather | solution.py:48
  55.9 54.2 %all-gather.9.cloned.1.call-done = bf16[2048,896]{1,0:T(8,128)(2,1)} async-done(((bf16[256,896]{1,0:T(8,128)(2,1)}), bf16[2048,896]{1,0:T(8,128)(2,1)}) %all-gather.9.cloned.1.call-update) | async-done | bytes 3670032 | tf_op jit(solution)/shard_map/all_gather | solution.py:54
  110.2 4.8 %convolution_bitcast_fusion = f32[1,512,896]{1,2,0:T(8,128)S(1)} fusion(bf16[2048,896]{1,0:T(8,128)(2,1)} %all-gather.9.cloned.1.call-done, bf16[512,2048]{1,0:T(8,128)(2,1)} %all-gather.7.cloned.1.call-done), kind=kOutput, calls=%fused_computation.8 | convolution fusion | flops 1879048192 | bytes 7602176 | tf_op jit(solution)/shard_map/dot_general | solution.py:24
  115.0 48.7 %all-gather.5.cloned.1.call-done = bf16[2048,896]{1,0:T(8,128)(2,1)} async-done(((bf16[256,896]{1,0:T(8,128)(2,1)}), bf16[2048,896]{1,0:T(8,128)(2,1)}) %all-gather.5.cloned.1.call-update) | async-done | bytes 3670032 | tf_op jit(solution)/shard_map/all_gather | solution.py:53
  163.7 4.8 %convolution_bitcast_fusion.1 = f32[1,512,896]{1,2,0:T(8,128)S(1)} fusion(bf16[2048,896]{1,0:T(8,128)(2,1)} %all-gather.5.cloned.1.call-done, bf16[512,2048]{1,0:T(8,128)(2,1)} %all-gather.7.cloned.1.call-done), kind=kOutput, calls=%fused_computation.9 | convolution fusion | flops 1879048192 | bytes 7602176 | tf_op jit(solution)/shard_map/dot_general | solution.py:24
  168.5 2.3 pad_maximum_fusion
  170.8 0.0 all-reduce.2.cloned.1.call-update
  170.9 0.0 reduce-scatter.2.cloned.1.call-start
  170.9 46.2 %all-gather.11.cloned.1.call-done = bf16[896,2048]{1,0:T(8,128)(2,1)} async-done(((bf16[112,2048]{1,0:T(8,128)(2,1)}), bf16[896,2048]{1,0:T(8,128)(2,1)}) %all-gather.11.cloned.1.call-update) | async-done | bytes 3670032 | tf_op jit(solution)/shard_map/all_gather | solution.py:58
  217.1 95.3 %all-reduce.2.cloned.1.call-done = f32[2,512,896]{1,2,0:T(8,128)} async-done(((f32[2,512,896]{1,2,0:T(8,128)}), f32[2,512,896]{1,2,0:T(8,128)}) %all-reduce.2.cloned.1.call-update) | async-done | bytes 3670032 | tf_op jit(solution)/shard_map/psum | solution.py:56
  312.4 7.7 %fusion.5 = f32[512,2048]{1,0:T(8,128)} fusion(bf16[896,2048]{1,0:T(8,128)(2,1)} %all-gather.11.cloned.1.call-done, f32[2,512,896]{1,2,0:T(8,128)} %all-reduce.2.cloned.1.call-done), kind=kOutput, calls=%fused_computation.16 | convolution fusion | flops 1881800704 | bytes 11534336 | tf_op jit(solution)/shard_map/dot_general | solution.py:60
  320.0 0.0 reduce-scatter.2.cloned.1.call-update
  320.1 65.3 %reduce-scatter.2.cloned.1.call-done = f32[32,2048]{1,0:T(8,128)} async-done(((f32[512,2048]{1,0:T(8,128)}), f32[32,2048]{1,0:T(8,128)}) %reduce-scatter.2.cloned.1.call-update) | async-done | bytes 262160 | tf_op jit(solution)/shard_map/reduce_scatter | solution.py:59
  385.4 1.6 convert_element_type.52
  (4 shorter events, 0.0 us)
Async XLA Ops:
  6.5 5.7 %copy-start = (bf16[112,2048]{1,0:T(8,128)(2,1)S(1)}, bf16[112,2048]{1,0:T(8,128)(2,1)}, u32[]{:S(2)}) copy-start(bf16[112,2048]{1,0:T(8,128)(2,1)} %param.10) | copy-start | bytes 1376260
  6.5 5.7 %copy-start.1 = (s32[112,64]{0,1:T(8,128)S(1)}, s32[112,64]{0,1:T(8,128)}, u32[]{:S(2)}) copy-start(s32[112,64]{0,1:T(8,128)} %param.13) | copy-start | bytes 86020
  6.5 49.4 %all-gather.7.cloned.1.call-start = ((), (), s32[]{:S(2)}) async-start(), calls=%async_computation.2 | async-start | bytes 2228224 | tf_op jit(solution)/shard_map/all_gather | solution.py:48
  7.3 102.9 %all-gather.9.cloned.1.call-start = ((), (), s32[]{:S(2)}) async-start(), calls=%async_computation.3 | async-start | bytes 4128768 | tf_op jit(solution)/shard_map/all_gather | solution.py:54
  9.7 154.0 %all-gather.5.cloned.1.call-start = ((), (), s32[]{:S(2)}) async-start(), calls=%async_computation.1 | async-start | bytes 4128768 | tf_op jit(solution)/shard_map/all_gather | solution.py:53
  12.1 205.0 %all-gather.11.cloned.1.call-start = ((), (), s32[]{:S(2)}) async-start(), calls=%async_computation.5 | async-start | bytes 4128768 | tf_op jit(solution)/shard_map/all_gather | solution.py:58
  13.7 298.7 %all-reduce.2.cloned.1.call-start = ((), (), s32[]{:S(2)}) async-start(), calls=%async_computation.4 | async-start | bytes 7340032 | tf_op jit(solution)/shard_map/psum | solution.py:56
  170.9 214.5 %reduce-scatter.2.cloned.1.call-start = ((), (), s32[]{:S(2)}) async-start(), calls=%async_computation.6 | async-start | bytes 4456448 | tf_op jit(solution)/shard_map/reduce_scatter | solution.py:59
Sparse Core Ops, SparseCore 0:
  9.5 46.3 all-gather.6
  58.0 52.1 all-gather.8
  112.2 51.4 all-gather.4
  165.6 51.3 all-gather.10
  219.3 93.0 all-reduce.1
  320.2 65.1 reduce-scatter.1
where the time goes:
time: 394 us
  waiting for transfers between devices  353 us (90%)
  matrix products  23.4 us (6%)
  between operations  13.5 us (3%)
  other arithmetic  4 us (1%)
    psum x1, waiting for transfers between devices, on_device(): total = lax.psum(both, 'depth')  95.3 us
    reduce_scatter x1, waiting for transfers between devices, on_device(): lax.psum_scatter(jnp.dot(hidden, down_block, preferred_element_type=jnp.f...  65.3 us
    all_gather x1, waiting for transfers between devices, on_device(): up = add_one(lax.all_gather(up_masked, 'row', axis=0, tiled=True))  54.2 us
    all_gather x1, waiting for transfers between devices, on_device(): gate = add_one(lax.all_gather(gate_masked, 'row', axis=0, tiled=True))  48.7 us
    all_gather x1, waiting for transfers between devices, on_device(): down_block = lax.all_gather(down_masked, 'row', axis=0, tiled=True)  46.2 us
    all_gather x1, waiting for transfers between devices, on_device(): token_block = lax.all_gather(tokens, 'col', axis=0, tiled=True)  42.2 us
    dot_general x2, matrix products, add_panel(): return jnp.dot(token_block, piece, preferred_element_type=jnp.float32)  9.61 us
  transfers between devices with their start and end apart: 6, of which 6 were waited for; matrix products, arithmetic and copies ran while one was open for 5% of the time, Pallas kernels for 0%

commit v1 on v0

--- a/solution.py
+++ b/solution.py
@@ -53,7 +53,7 @@
     gate = add_one(lax.all_gather(gate_masked, "row", axis=0, tiled=True))
     up = add_one(lax.all_gather(up_masked, "row", axis=0, tiled=True))
     both = jnp.stack((gate, up), 0)
-    total = lax.psum(both, "depth")
+    total = jnp.sum(lax.all_gather(both, "depth"), axis=0)
     hidden = (jax.nn.silu(total[0]) * total[1]).astype(jnp.bfloat16)
     down_block = lax.all_gather(down_masked, "row", axis=0, tiled=True)
     mixed = lax.psum_scatter(

time: 394 us -> 452 us (1.15)
  the two profiles are of different devices: /device:TPU:25 before, /device:TPU:4 now
where the time goes in v1:
time: 452 us; the launch traced here: 451 us
  waiting for transfers between devices  388 us (86%)
  matrix products  23.3 us (5%)
  local copies, waits for them, and re-layouts  13.6 us (3%)
  between operations  13.5 us (3%)
  other arithmetic  12.1 us (3%)
    all_gather x1, waiting for transfers between devices, on_device(): total = jnp.sum(lax.all_gather(both, 'depth'), axis=0)  137 us
    reduce_scatter x1, waiting for transfers between devices, on_device(): lax.psum_scatter(jnp.dot(hidden, down_block, preferred_element_type=jnp.f...  63.3 us
    all_gather x1, waiting for transfers between devices, on_device(): up = add_one(lax.all_gather(up_masked, 'row', axis=0, tiled=True))  54.4 us
    all_gather x1, waiting for transfers between devices, on_device(): gate = add_one(lax.all_gather(gate_masked, 'row', axis=0, tiled=True))  48.7 us
    all_gather x1, waiting for transfers between devices, on_device(): token_block = lax.all_gather(tokens, 'col', axis=0, tiled=True)  43.9 us
    all_gather x1, waiting for transfers between devices, on_device(): down_block = lax.all_gather(down_masked, 'row', axis=0, tiled=True)  40.3 us
    dot_general x2, matrix products, add_panel(): return jnp.dot(token_block, piece, preferred_element_type=jnp.float32)  9.61 us
  transfers between devices with their start and end apart: 6, of which 6 were waited for; matrix products, arithmetic and copies ran while one was open for 6% of the time, Pallas kernels for 0%

profile of v1, /device:TPU:4, one launch (start us, length us, event | category | flops | bytes accessed | tf_op | source)
XLA Modules:
  0.0 451.2 jit_solution(15507913701998366720)
XLA Ops:
  6.5 0.0 all-gather.9.cloned.1.call-start
  6.5 0.7 all-gather.9.cloned.1.call-update
  7.3 0.0 all-gather.11.cloned.1.call-start
  7.3 2.4 fusion.6
  9.7 0.0 all-gather.11.cloned.1.call-update
  9.7 0.0 all-gather.7.cloned.1.call-start
  9.8 2.3 fusion.5
  12.1 0.0 all-gather.7.cloned.1.call-update
  12.1 0.0 all-gather.15.cloned.1.call-start
  12.2 43.9 %all-gather.9.cloned.1.call-done = bf16[512,2048]{1,0:T(8,128)(2,1)} async-done(((bf16[32,2048]{1,0:T(8,128)(2,1)}), bf16[512,2048]{1,0:T(8,128)(2,1)}) %all-gather.9.cloned.1.call-update) | async-done | bytes 2097168 | tf_op jit(solution)/shard_map/all_gather | solution.py:48
  56.0 54.4 %all-gather.11.cloned.1.call-done = bf16[2048,896]{1,0:T(8,128)(2,1)} async-done(((bf16[256,896]{1,0:T(8,128)(2,1)}), bf16[2048,896]{1,0:T(8,128)(2,1)}) %all-gather.11.cloned.1.call-update) | async-done | bytes 3670032 | tf_op jit(solution)/shard_map/all_gather | solution.py:54
  110.4 4.8 %convolution_bitcast_fusion = f32[1,512,896]{1,2,0:T(8,128)S(1)} fusion(bf16[2048,896]{1,0:T(8,128)(2,1)} %all-gather.11.cloned.1.call-done, bf16[512,2048]{1,0:T(8,128)(2,1)} %all-gather.9.cloned.1.call-done), kind=kOutput, calls=%fused_computation.11 | convolution fusion | flops 1879048192 | bytes 7602176 | tf_op jit(solution)/shard_map/dot_general | solution.py:24
  115.2 48.7 %all-gather.7.cloned.1.call-done = bf16[2048,896]{1,0:T(8,128)(2,1)} async-done(((bf16[256,896]{1,0:T(8,128)(2,1)}), bf16[2048,896]{1,0:T(8,128)(2,1)}) %all-gather.7.cloned.1.call-update) | async-done | bytes 3670032 | tf_op jit(solution)/shard_map/all_gather | solution.py:53
  163.9 4.8 %convolution_bitcast_fusion.1 = f32[1,512,896]{1,2,0:T(8,128)S(1)} fusion(bf16[2048,896]{1,0:T(8,128)(2,1)} %all-gather.7.cloned.1.call-done, bf16[512,2048]{1,0:T(8,128)(2,1)} %all-gather.9.cloned.1.call-done), kind=kOutput, calls=%fused_computation.12 | convolution fusion | flops 1879048192 | bytes 7602176 | tf_op jit(solution)/shard_map/dot_general | solution.py:24
  168.7 2.2 pad_maximum_fusion
  170.9 4.6 %copy.8 = f32[2,512,896]{2,1,0:T(8,128)} copy(f32[2,512,896]{1,2,0:T(8,128)} %pad_maximum_fusion) | data formatting | bytes 7340032 | tf_op jit(solution)/shard_map/stack | solution.py:55
  175.6 0.0 copy-start
  175.6 0.0 copy-start.1
  175.6 0.0 all-gather.15.cloned.1.call-update
  175.6 0.0 all-gather.13.cloned.1.call-start
  175.7 0.9 copy-done
  176.6 0.0 copy-done.1
  176.6 1.5 fusion
  178.1 0.0 all-gather.13.cloned.1.call-update
  178.1 0.0 reduce-scatter.2.cloned.1.call-start
  178.1 137.1 %all-gather.15.cloned.1.call-done = f32[8,512,896]{2,1,0:T(8,128)} async-done(((f32[2,512,896]{2,1,0:T(8,128)}), f32[8,512,896]{2,1,0:T(8,128)}) %all-gather.15.cloned.1.call-update) | async-done | bytes 14680080 | tf_op jit(solution)/shard_map/all_gather | solution.py:56
  315.2 8.2 %reduce_sum.9 = f32[2,512,896]{2,1,0:T(8,128)} reduce(f32[4,2,512,896]{3,2,1,0:T(8,128)} %bitcast.33, f32[]{:T(128)} %constant.73.clone.1), dimensions={0}, to_apply=%region_0.1 | reduce | flops 2752512 | bytes 18350084 | tf_op jit(solution)/shard_map/reduce_sum | solution.py:56
  323.4 3.6 fusion.37
  327.0 2.8 copy.11
  329.8 1.7 copy.12
  331.5 40.3 %all-gather.13.cloned.1.call-done = bf16[896,2048]{1,0:T(8,128)(2,1)} async-done(((bf16[112,2048]{1,0:T(8,128)(2,1)}), bf16[896,2048]{1,0:T(8,128)(2,1)}) %all-gather.13.cloned.1.call-update) | async-done | bytes 3670032 | tf_op jit(solution)/shard_map/all_gather | solution.py:58
  371.8 7.6 %fusion.7 = f32[512,2048]{1,0:T(8,128)} fusion(bf16[896,2048]{1,0:T(8,128)(2,1)} %all-gather.13.cloned.1.call-done, f32[1,512,896]{1,2,0:T(8,128)} %copy.12, f32[1,512,896]{1,2,0:T(8,128)} %copy.11), kind=kOutput, calls=%fused_computation.19 | convolution fusion | flops 1881800704 | bytes 11534336 | tf_op jit(solution)/shard_map/dot_general | solution.py:60
  379.4 0.0 reduce-scatter.2.cloned.1.call-update
  379.4 63.3 %reduce-scatter.2.cloned.1.call-done = f32[32,2048]{1,0:T(8,128)} async-done(((f32[512,2048]{1,0:T(8,128)}), f32[32,2048]{1,0:T(8,128)}) %reduce-scatter.2.cloned.1.call-update) | async-done | bytes 262160 | tf_op jit(solution)/shard_map/reduce_scatter | solution.py:59
  442.8 1.6 convert_element_type.52
  (4 shorter events, 0.0 us)
Async XLA Ops:
  6.5 49.5 %all-gather.9.cloned.1.call-start = ((), (), s32[]{:S(2)}) async-start(), calls=%async_computation.2 | async-start | bytes 2228224 | tf_op jit(solution)/shard_map/all_gather | solution.py:48
  7.3 103.1 %all-gather.11.cloned.1.call-start = ((), (), s32[]{:S(2)}) async-start(), calls=%async_computation.3 | async-start | bytes 4128768 | tf_op jit(solution)/shard_map/all_gather | solution.py:54
  9.7 154.2 %all-gather.7.cloned.1.call-start = ((), (), s32[]{:S(2)}) async-start(), calls=%async_computation.1 | async-start | bytes 4128768 | tf_op jit(solution)/shard_map/all_gather | solution.py:53
  12.1 303.1 %all-gather.15.cloned.1.call-start = ((), (), s32[]{:S(2)}) async-start(), calls=%async_computation.6 | async-start | bytes 18350080 | tf_op jit(solution)/shard_map/all_gather | solution.py:56
  175.6 1.0 copy-start
  175.6 1.0 copy-start.1
  175.6 196.2 %all-gather.13.cloned.1.call-start = ((), (), s32[]{:S(2)}) async-start(), calls=%async_computation.4 | async-start | bytes 4128768 | tf_op jit(solution)/shard_map/all_gather | solution.py:58
  178.1 264.7 %reduce-scatter.2.cloned.1.call-start = ((), (), s32[]{:S(2)}) async-start(), calls=%async_computation.5 | async-start | bytes 4456448 | tf_op jit(solution)/shard_map/reduce_scatter | solution.py:59
Sparse Core Ops, SparseCore 0:
  9.5 46.5 all-gather.8
  58.1 52.2 all-gather.10
  112.5 51.3 all-gather.6
  175.7 139.4 all-gather.14
  317.1 54.6 all-gather.12
  379.5 63.1 reduce-scatter.1
